TPU v7x, 32 devices: a whole 2x2x4 slice. The times are simulated.
32 devices in a mesh: row: 8 (over y, x, core), col: 4 (over z).
Axes of the slice: x: 2, y: 2, z: 4, core: 2. Of those that a mesh axis runs over, the one named last changes fastest.
Arguments:
- front_first: float32 [8, 8, 128, 4, 16, 128], P('row', None, None, 'col'), as said below
- front_second: float32 [8, 8, 128, 4, 16, 128], P('row', None, None, 'col'), as said below
- front_third: float32 [8, 8, 128, 4, 16, 128], P('row', None, None, 'col'), as said below
- map_second: int32 [60], replicated, may hold values from 0 to 63, as said below
- map_third: int32 [60], replicated, may hold values from 0 to 63, as said below
Outputs:
- lower_first: float32 [8, 8, 128, 512], P('row')
- lower_second: float32 [8, 8, 128, 512], P('row')
- lower_third: float32 [8, 8, 128, 512], P('row')
- schur_third: float32 [8, 8, 128, 4, 16, 128], P('row', None, None, 'col')
Inputs may be any that keep to these rules, and one draw needn't show every extreme that they name: `map_second`: strictly increasing; the first entry is 0 and the last is 63. `map_third`: strictly increasing; the first entry is 0 and the last is 63. `front_first`: symmetric positive definite. `front_second`: symmetric positive definite. `front_third`: symmetric positive definite.
All inputs are finite; a program needn't handle non-finite values.
Results may differ from a plain program's by a relative error of at most 0.00012.
Values sent between devices are 32-bit elements; how exact they have to be, the bound alone decides.
A program may use at most 128 MiB of HBM per device.

v0:
```python
import jax
import jax.numpy as jnp
from jax import lax
from jax.sharding import PartitionSpec as P

TILE = 128
PANEL = 512
PIVOTS = 512


def shifted(value, axis, steps):
    count = lax.axis_size(axis)
    pairs = [(source, (source + steps) % count) for source in range(count)]
    return lax.ppermute(value, axis, pairs)


def spread(block, axis, source):
    block = jnp.where(lax.axis_index(axis) == source, block, jnp.zeros_like(block))
    return lax.psum(block, axis)


def shift_rows(block_data, amount):
    return shifted(block_data, "row", amount)


def shift_cols(block_data, amount):
    return shifted(block_data, "col", amount)


def relocate(block_data, block_map, axis_dim, count, index, shifter):
    pivot_blocks = PIVOTS // TILE
    local_tiles = block_data.shape[axis_dim]
    child_start = jnp.arange(block_map.shape[0], dtype=jnp.int32) + pivot_blocks
    displacement = child_start - block_map
    local_pos = jnp.arange(local_tiles, dtype=jnp.int32) * count + index
    for bit_index in reversed(range(pivot_blocks.bit_length())):
        stride = 1 << bit_index
        high_part = displacement >> bit_index + 1 << bit_index + 1
        where_now = child_start - high_part
        moving_now = displacement >> bit_index & 1 == 1
        moving = jnp.any((where_now[None, :] == local_pos[:, None]) & moving_now[None, :], axis=1)
        if axis_dim == 0:
            tile_mask = moving[:, None, None, None]
        else:
            tile_mask = moving[None, None, :, None]
        sending = jnp.where(tile_mask, block_data, 0.0)
        staying = jnp.where(tile_mask, 0.0, block_data)
        full_turns = stride // count
        remainder = stride % count
        if remainder:
            arrived = shifter(sending, count - remainder)
        else:
            arrived = sending
        roll_amount = full_turns + (index + remainder >= count).astype(jnp.int32)
        arrived = jnp.roll(arrived, -roll_amount, axis=axis_dim)
        block_data = staying + arrived
    return block_data


def per_device(front_first, front_second, front_third, map_second, map_third):
    row_count = lax.axis_size("row")
    col_count = lax.axis_size("col")
    row_index = lax.axis_index("row")
    col_index = lax.axis_index("col")
    tiles_row = front_first.shape[1]
    tile_size = front_first.shape[2]
    tiles_col = front_first.shape[4]
    panel_tiles = PANEL // tile_size
    row_logical = (
        (jnp.arange(tiles_row, dtype=jnp.int32) * row_count + row_index)[:, None] * tile_size
        + jnp.arange(tile_size, dtype=jnp.int32)[None, :]
    ).reshape(-1)
    col_logical = (
        (jnp.arange(tiles_col, dtype=jnp.int32) * col_count + col_index)[:, None] * tile_size
        + jnp.arange(tile_size, dtype=jnp.int32)[None, :]
    ).reshape(-1)

    def local_form(front):
        return front.reshape(tiles_row, tile_size, tiles_col, tile_size)

    def factor_local(matrix):
        first_tile = 0 // tile_size
        pieces = []
        for member in range(panel_tiles):
            global_col = first_tile + member
            pieces.append(
                spread(matrix[:, :, global_col // col_count, :], "col", global_col % col_count)
            )
        panel_cols = jnp.stack(pieces, axis=2).reshape(tiles_row * tile_size, PANEL)
        panel_tiled = panel_cols.reshape(tiles_row, tile_size, PANEL)
        diagonal_parts = []
        for member in range(panel_tiles):
            global_row = first_tile + member
            diagonal_parts.append(
                spread(panel_tiled[global_row // row_count], "row", global_row % row_count)
            )
        diagonal = jnp.concatenate(diagonal_parts, axis=0)
        factor_block = jnp.linalg.cholesky(diagonal)
        inverse = lax.linalg.triangular_solve(
            factor_block, jnp.eye(PANEL, dtype=jnp.float32), left_side=True, lower=True
        )
        lower_panel = jnp.dot(
            panel_cols,
            inverse.T,
            precision=lax.Precision.HIGHEST,
            preferred_element_type=jnp.float32,
        )
        lower_panel = jnp.where((row_logical >= 0)[:, None], lower_panel, 0.0)
        received = []
        for member in range(row_count // col_count):
            got = spread(lower_panel, "row", member * col_count + col_index)
            received.append(got.reshape(tiles_row, tile_size, PANEL))
        column_side = jnp.stack(received, axis=1).reshape(tiles_col * tile_size, PANEL)
        update = jnp.dot(
            lower_panel,
            column_side.T,
            precision=lax.Precision.HIGHEST,
            preferred_element_type=jnp.float32,
        )
        matrix = matrix - update.reshape(tiles_row, tile_size, tiles_col, tile_size)
        row_keep = (row_logical >= PIVOTS).reshape(tiles_row, tile_size)
        col_keep = (col_logical >= PIVOTS).reshape(tiles_col, tile_size)
        schur = jnp.where(row_keep[:, :, None, None] & col_keep[None, None, :, :], matrix, 0.0)
        return (lower_panel, schur)

    def extend_local(parent, schur, block_map):
        moved = relocate(schur, block_map, 0, row_count, row_index, shift_rows)
        moved = relocate(moved, block_map, 2, col_count, col_index, shift_cols)
        return parent + moved

    lower_first, schur_first = factor_local(local_form(front_first))
    lower_second, schur_second = factor_local(
        extend_local(local_form(front_second), schur_first, map_second)
    )
    lower_third, schur_third = factor_local(
        extend_local(local_form(front_third), schur_second, map_third)
    )
    out_shape = (1, tiles_row, tile_size, PIVOTS)
    return (
        lower_first.reshape(out_shape),
        lower_second.reshape(out_shape),
        lower_third.reshape(out_shape),
        schur_third.reshape(1, tiles_row, tile_size, 1, tiles_col, tile_size),
    )


def solution(mesh):
    return jax.shard_map(
        per_device,
        mesh=mesh,
        in_specs=(
            P("row", None, None, "col", None, None),
            P("row", None, None, "col", None, None),
            P("row", None, None, "col", None, None),
            P(),
            P(),
        ),
        out_specs=(
            P("row", None, None, None),
            P("row", None, None, None),
            P("row", None, None, None),
            P("row", None, None, "col", None, None),
        ),
        check_vma=False,
    )
```

profile of v0, /device:TPU:0, one launch (start us, length us, event | category | flops | bytes accessed | tf_op | source)
XLA Modules:
  0.0 3451.2 jit_solution(5352810742912284232)
XLA Ops:
  19.0 90.8 %all-reduce.36.cloned.1.call-done = (f32[8,128,1,128]{3,1,2,0:T(8,128)}, f32[8,128,1,128]{3,1,2,0:T(8,128)}, f32[8,128,1,128]{3,1,2,0:T(8,128)}, f32[8,128,1,128]{3,1,2,0:T(8,128)}) async-done(((f32[8,128,1,128]{3,1,2,0:T(8,128)}, f32[8,128,1,128]{3,1,2,0:T(8,128)}, f32[8,128,1,128]{3,1,2,0:T(8,128)}, f32[8,128,1,128]{3,1,2,0:T(8,128)}), (f32[8,128,1,128]{3,1,2,0:T(8,128)}, f32[8,128,1,128]{3,1,2,0:T(8,128)}, ...) | async-done | bytes 2097168 | tf_op jit(solution)/shard_map/psum | solution.py:19
  121.7 53.2 %all-reduce.30.cloned.1.call-done = (f32[128,512]{0,1:T(8,128)}, f32[128,512]{0,1:T(8,128)}, f32[128,512]{0,1:T(8,128)}, f32[128,512]{0,1:T(8,128)}) async-done(((f32[128,512]{0,1:T(8,128)}, f32[128,512]{0,1:T(8,128)}, f32[128,512]{0,1:T(8,128)}, f32[128,512]{0,1:T(8,128)}), (f32[128,512]{0,1:T(8,128)}, f32[128,512]{0,1:T(8,128)}, f32[128,512]{0,1:T(8,128)}, ...) | async-done | bytes 1048592 | tf_op jit(solution)/shard_map/psum | solution.py:19
  293.7 40.1 %custom-call.34 = f32[4,128,128]{1,2,0:T(8,128)S(1)} custom-call(f32[4,128,128]{2,1,0:T(8,128)} %copy-done.12), custom_call_target="InvertDiagBlocksLowerTriangular" | custom-call | tf_op jit(solution)/shard_map/triangular_solve/custom-call.3 | solution.py:99
  349.4 80.1 %all-reduce.28.cloned.1.call-done = (f32[8,1,128,512]{3,2,0,1:T(8,128)}, f32[8,1,128,512]{3,2,0,1:T(8,128)}) async-done(((f32[8,1,128,512]{3,2,0,1:T(8,128)}, f32[8,1,128,512]{3,2,0,1:T(8,128)}), (f32[8,1,128,512]{3,2,0,1:T(8,128)}, f32[8,1,128,512]{3,2,0,1:T(8,128)})) %all-reduce.28.cloned.1.call-update) | async-done | bytes 4194320 | tf_op jit(solution)/shard_map/psum | solution.py:19
  435.0 21.4 broadcast_select_fusion.11
  457.7 181.1 %collective-permute-done = f32[8,128,16,128]{3,1,2,0:T(8,128)} collective-permute-done((f32[8,128,16,128]{3,1,2,0:T(8,128)}, f32[8,128,16,128]{3,1,2,0:T(8,128)}, u32[]{:S(2)}, u32[]{:S(2)}) %collective-permute-start) | collective-permute-done | bytes 8388640 | tf_op jit(solution)/shard_map/ppermute | solution.py:14
  652.4 179.9 %collective-permute-done.1 = f32[8,128,16,128]{3,1,2,0:T(8,128)} collective-permute-done((f32[8,128,16,128]{3,1,2,0:T(8,128)}, f32[8,128,16,128]{3,1,2,0:T(8,128)}, u32[]{:S(2)}, u32[]{:S(2)}) %collective-permute-start.1) | collective-permute-done | bytes 8388640 | tf_op jit(solution)/shard_map/ppermute | solution.py:14
  844.8 91.0 %collective-permute-done.2 = f32[8,128,16,128]{3,1,2,0:T(8,128)} collective-permute-done((f32[8,128,16,128]{3,1,2,0:T(8,128)}, f32[8,128,16,128]{3,1,2,0:T(8,128)}, u32[]{:S(2)}, u32[]{:S(2)}) %collective-permute-start.2) | collective-permute-done | bytes 8388640 | tf_op jit(solution)/shard_map/ppermute | solution.py:14
  958.1 360.9 %collective-permute-done.3 = f32[8,128,16,128]{3,1,2,0:T(8,128)} collective-permute-done((f32[8,128,16,128]{3,1,2,0:T(8,128)}, f32[8,128,16,128]{3,1,2,0:T(8,128)}, u32[]{:S(2)}, u32[]{:S(2)}) %collective-permute-start.3) | collective-permute-done | bytes 8388640 | tf_op jit(solution)/shard_map/ppermute | solution.py:14
  1335.1 180.3 %collective-permute-done.4 = f32[8,128,16,128]{3,1,2,0:T(8,128)} collective-permute-done((f32[8,128,16,128]{3,1,2,0:T(8,128)}, f32[8,128,16,128]{3,1,2,0:T(8,128)}, u32[]{:S(2)}, u32[]{:S(2)}) %collective-permute-start.4) | collective-permute-done | bytes 8388640 | tf_op jit(solution)/shard_map/ppermute | solution.py:14
  1530.7 89.9 %all-reduce.34.cloned.1.call-done = (f32[8,128,1,128]{3,1,2,0:T(8,128)}, f32[8,128,1,128]{3,1,2,0:T(8,128)}, f32[8,128,1,128]{3,1,2,0:T(8,128)}, f32[8,128,1,128]{3,1,2,0:T(8,128)}) async-done(((f32[8,128,1,128]{3,1,2,0:T(8,128)}, f32[8,128,1,128]{3,1,2,0:T(8,128)}, f32[8,128,1,128]{3,1,2,0:T(8,128)}, f32[8,128,1,128]{3,1,2,0:T(8,128)}), (f32[8,128,1,128]{3,1,2,0:T(8,128)}, f32[8,128,1,128]{3,1,2,0:T(8,128)}, ...) | async-done | bytes 2097168 | tf_op jit(solution)/shard_map/psum | solution.py:19
  1634.2 53.9 %all-reduce.26.cloned.1.call-done = (f32[128,512]{0,1:T(8,128)}, f32[128,512]{0,1:T(8,128)}, f32[128,512]{0,1:T(8,128)}, f32[128,512]{0,1:T(8,128)}) async-done(((f32[128,512]{0,1:T(8,128)}, f32[128,512]{0,1:T(8,128)}, f32[128,512]{0,1:T(8,128)}, f32[128,512]{0,1:T(8,128)}), (f32[128,512]{0,1:T(8,128)}, f32[128,512]{0,1:T(8,128)}, f32[128,512]{0,1:T(8,128)}, ...) | async-done | bytes 1048592 | tf_op jit(solution)/shard_map/psum | solution.py:19
  1790.1 39.3 %custom-call.38 = f32[4,128,128]{1,2,0:T(8,128)S(1)} custom-call(f32[4,128,128]{2,1,0:T(8,128)S(1)} %get-tuple-element.29), custom_call_target="InvertDiagBlocksLowerTriangular" | custom-call | tf_op jit(solution)/shard_map/triangular_solve/custom-call.3 | solution.py:99
  1843.4 80.3 %all-reduce.24.cloned.1.call-done = (f32[8,1,128,512]{3,2,0,1:T(8,128)}, f32[8,1,128,512]{3,2,0,1:T(8,128)}) async-done(((f32[8,1,128,512]{3,2,0,1:T(8,128)}, f32[8,1,128,512]{3,2,0,1:T(8,128)}), (f32[8,1,128,512]{3,2,0,1:T(8,128)}, f32[8,1,128,512]{3,2,0,1:T(8,128)})) %all-reduce.24.cloned.1.call-update) | async-done | bytes 4194320 | tf_op jit(solution)/shard_map/psum | solution.py:19
  1928.9 15.6 broadcast_select_fusion.5
  1945.9 180.8 %collective-permute-done.5 = f32[8,128,16,128]{3,1,2,0:T(8,128)S(1)} collective-permute-done((f32[8,128,16,128]{3,1,2,0:T(8,128)S(1)}, f32[8,128,16,128]{3,1,2,0:T(8,128)S(1)}, u32[]{:S(2)}, u32[]{:S(2)}) %collective-permute-start.5) | collective-permute-done | bytes 8388640 | tf_op jit(solution)/shard_map/ppermute | solution.py:14
  2141.7 179.8 %collective-permute-done.6 = f32[8,128,16,128]{3,1,2,0:T(8,128)S(1)} collective-permute-done((f32[8,128,16,128]{3,1,2,0:T(8,128)}, f32[8,128,16,128]{3,1,2,0:T(8,128)S(1)}, u32[]{:S(2)}, u32[]{:S(2)}) %collective-permute-start.6) | collective-permute-done | bytes 8388640 | tf_op jit(solution)/shard_map/ppermute | solution.py:14
  2335.3 91.3 %collective-permute-done.7 = f32[8,128,16,128]{3,1,2,0:T(8,128)} collective-permute-done((f32[8,128,16,128]{3,1,2,0:T(8,128)}, f32[8,128,16,128]{3,1,2,0:T(8,128)}, u32[]{:S(2)}, u32[]{:S(2)}) %collective-permute-start.7) | collective-permute-done | bytes 8388640 | tf_op jit(solution)/shard_map/ppermute | solution.py:14
  2449.0 360.8 %collective-permute-done.8 = f32[8,128,16,128]{3,1,2,0:T(8,128)} collective-permute-done((f32[8,128,16,128]{3,1,2,0:T(8,128)}, f32[8,128,16,128]{3,1,2,0:T(8,128)}, u32[]{:S(2)}, u32[]{:S(2)}) %collective-permute-start.8) | collective-permute-done | bytes 8388640 | tf_op jit(solution)/shard_map/ppermute | solution.py:14
  2824.2 180.3 %collective-permute-done.9 = f32[8,128,16,128]{3,1,2,0:T(8,128)S(1)} collective-permute-done((f32[8,128,16,128]{3,1,2,0:T(8,128)}, f32[8,128,16,128]{3,1,2,0:T(8,128)S(1)}, u32[]{:S(2)}, u32[]{:S(2)}) %collective-permute-start.9) | collective-permute-done | bytes 8388640 | tf_op jit(solution)/shard_map/ppermute | solution.py:14
  3023.3 89.8 %all-reduce.32.cloned.1.call-done = (f32[8,128,1,128]{3,1,2,0:T(8,128)}, f32[8,128,1,128]{3,1,2,0:T(8,128)}, f32[8,128,1,128]{3,1,2,0:T(8,128)}, f32[8,128,1,128]{3,1,2,0:T(8,128)}) async-done(((f32[8,128,1,128]{3,1,2,0:T(8,128)}, f32[8,128,1,128]{3,1,2,0:T(8,128)}, f32[8,128,1,128]{3,1,2,0:T(8,128)}, f32[8,128,1,128]{3,1,2,0:T(8,128)}), (f32[8,128,1,128]{3,1,2,0:T(8,128)}, f32[8,128,1,128]{3,1,2,0:T(8,128)}, ...) | async-done | bytes 2097168 | tf_op jit(solution)/shard_map/psum | solution.py:19
  3126.6 53.9 %all-reduce.22.cloned.1.call-done = (f32[128,512]{0,1:T(8,128)}, f32[128,512]{0,1:T(8,128)}, f32[128,512]{0,1:T(8,128)}, f32[128,512]{0,1:T(8,128)}) async-done(((f32[128,512]{0,1:T(8,128)}, f32[128,512]{0,1:T(8,128)}, f32[128,512]{0,1:T(8,128)}, f32[128,512]{0,1:T(8,128)}), (f32[128,512]{0,1:T(8,128)}, f32[128,512]{0,1:T(8,128)}, f32[128,512]{0,1:T(8,128)}, ...) | async-done | bytes 1048592 | tf_op jit(solution)/shard_map/psum | solution.py:19
  3282.2 39.3 %custom-call.42 = f32[4,128,128]{1,2,0:T(8,128)S(1)} custom-call(f32[4,128,128]{2,1,0:T(8,128)S(1)} %get-tuple-element.30), custom_call_target="InvertDiagBlocksLowerTriangular" | custom-call | tf_op jit(solution)/shard_map/triangular_solve/custom-call.3 | solution.py:99
  3335.5 80.5 %all-reduce.20.cloned.1.call-done = (f32[8,1,128,512]{3,2,0,1:T(8,128)}, f32[8,1,128,512]{3,2,0,1:T(8,128)}) async-done(((f32[8,1,128,512]{3,2,0,1:T(8,128)}, f32[8,1,128,512]{3,2,0,1:T(8,128)}), (f32[8,1,128,512]{3,2,0,1:T(8,128)}, f32[8,1,128,512]{3,2,0,1:T(8,128)})) %all-reduce.20.cloned.1.call-update) | async-done | bytes 4194320 | tf_op jit(solution)/shard_map/psum | solution.py:19
  (299 shorter events, 641.8 us)
Async XLA Ops:
  7.2 102.7 %all-reduce.36.cloned.1.call-start = ((), (), s32[]{:S(2)}) async-start(), calls=%async_computation.8 | async-start | bytes 4194304 | tf_op jit(solution)/shard_map/psum | solution.py:19
  18.9 156.0 %all-reduce.30.cloned.1.call-start = ((), (), s32[]{:S(2)}) async-start(), calls=%async_computation.5 | async-start | bytes 2097152 | tf_op jit(solution)/shard_map/psum | solution.py:19
  119.0 310.5 %all-reduce.28.cloned.1.call-start = ((), (), s32[]{:S(2)}) async-start(), calls=%async_computation.4 | async-start | bytes 8388608 | tf_op jit(solution)/shard_map/psum | solution.py:19
  337.2 11.8 copy-start.13
  337.2 11.8 copy-start.14
  348.9 1271.8 %all-reduce.34.cloned.1.call-start = ((), (), s32[]{:S(2)}) async-start(), calls=%async_computation.7 | async-start | bytes 4194304 | tf_op jit(solution)/shard_map/psum | solution.py:19
  429.4 4.1 copy-start.7
  456.4 182.4 %collective-permute-start = (f32[8,128,16,128]{3,1,2,0:T(8,128)}, f32[8,128,16,128]{3,1,2,0:T(8,128)}, u32[]{:S(2)}, u32[]{:S(2)}) collective-permute-start(f32[8,128,16,128]{3,1,2,0:T(8,128)} %get-tuple-element.212), channel_id=1, source_target_pairs={{0,16},{4,20},{8,24},{12,28},{16,0},{20,4},{24,8},{28,12},{1,17},{... | collective-permute-start | bytes 25165832 | tf_op jit(solution)/shard_map/ppermute | solution.py:14
  650.7 181.6 %collective-permute-start.1 = (f32[8,128,16,128]{3,1,2,0:T(8,128)}, f32[8,128,16,128]{3,1,2,0:T(8,128)}, u32[]{:S(2)}, u32[]{:S(2)}) collective-permute-start(f32[8,128,16,128]{3,1,2,0:T(8,128)} %get-tuple-element.127), channel_id=1, source_target_pairs={{0,24},{4,28},{8,0},{12,4},{16,8},{20,12},{24,16},{28,20},{1,25},{... | collective-permute-start | bytes 25165832 | tf_op jit(solution)/shard_map/ppermute | solution.py:14
  844.1 91.8 %collective-permute-start.2 = (f32[8,128,16,128]{3,1,2,0:T(8,128)}, f32[8,128,16,128]{3,1,2,0:T(8,128)}, u32[]{:S(2)}, u32[]{:S(2)}) collective-permute-start(f32[8,128,16,128]{3,1,2,0:T(8,128)} %get-tuple-element.125), channel_id=1, source_target_pairs={{0,28},{4,0},{8,4},{12,8},{16,12},{20,16},{24,20},{28,24},{1,29},{... | collective-permute-start | bytes 25165832 | tf_op jit(solution)/shard_map/ppermute | solution.py:14
  955.7 363.3 %collective-permute-start.3 = (f32[8,128,16,128]{3,1,2,0:T(8,128)}, f32[8,128,16,128]{3,1,2,0:T(8,128)}, u32[]{:S(2)}, u32[]{:S(2)}) collective-permute-start(f32[8,128,16,128]{3,1,2,0:T(8,128)} %get-tuple-element.121), channel_id=1, source_target_pairs={{0,2},{1,3},{2,0},{3,1},{4,6},{5,7},{6,4},{7,5},{8,10},{9,11},{10,... | collective-permute-start | bytes 25165832 | tf_op jit(solution)/shard_map/ppermute | solution.py:14
  1330.8 184.6 %collective-permute-start.4 = (f32[8,128,16,128]{3,1,2,0:T(8,128)}, f32[8,128,16,128]{3,1,2,0:T(8,128)}, u32[]{:S(2)}, u32[]{:S(2)}) collective-permute-start(f32[8,128,16,128]{3,1,2,0:T(8,128)} %get-tuple-element.119), channel_id=1, source_target_pairs={{0,3},{1,0},{2,1},{3,2},{4,7},{5,4},{6,5},{7,6},{8,11},{9,8},{10,9... | collective-permute-start | bytes 25165832 | tf_op jit(solution)/shard_map/ppermute | solution.py:14
  1530.7 157.5 %all-reduce.26.cloned.1.call-start = ((), (), s32[]{:S(2)}) async-start(), calls=%async_computation.3 | async-start | bytes 2097152 | tf_op jit(solution)/shard_map/psum | solution.py:19
  1632.1 291.6 %all-reduce.24.cloned.1.call-start = ((), (), s32[]{:S(2)}) async-start(), calls=%async_computation.2 | async-start | bytes 8388608 | tf_op jit(solution)/shard_map/psum | solution.py:19
  1843.1 84.1 %copy-start.2 = (f32[1024,512]{1,0:T(8,128)}, f32[1024,512]{1,0:T(8,128)S(1)}, u32[]{:S(2)}) copy-start(f32[1024,512]{1,0:T(8,128)S(1)} %get-tuple-element.216) | copy-start | bytes 6291460
  1843.2 1269.9 %all-reduce.32.cloned.1.call-start = ((), (), s32[]{:S(2)}) async-start(), calls=%async_computation.6 | async-start | bytes 4194304 | tf_op jit(solution)/shard_map/psum | solution.py:19
  1944.5 182.2 %collective-permute-start.5 = (f32[8,128,16,128]{3,1,2,0:T(8,128)S(1)}, f32[8,128,16,128]{3,1,2,0:T(8,128)S(1)}, u32[]{:S(2)}, u32[]{:S(2)}) collective-permute-start(f32[8,128,16,128]{3,1,2,0:T(8,128)S(1)} %get-tuple-element.217), channel_id=1, source_target_pairs={{0,16},{4,20},{8,24},{12,28},{16,0},{20,4},{24,8},{28,12},{1,17},{... | collective-permute-start | bytes 25165832 | tf_op jit(solution)/shard_map/ppermute | solution.py:14
  2140.0 181.5 %collective-permute-start.6 = (f32[8,128,16,128]{3,1,2,0:T(8,128)}, f32[8,128,16,128]{3,1,2,0:T(8,128)S(1)}, u32[]{:S(2)}, u32[]{:S(2)}) collective-permute-start(f32[8,128,16,128]{3,1,2,0:T(8,128)} %get-tuple-element.117), channel_id=1, source_target_pairs={{0,24},{4,28},{8,0},{12,4},{16,8},{20,12},{24,16},{28,20},{1,25},{... | collective-permute-start | bytes 25165832 | tf_op jit(solution)/shard_map/ppermute | solution.py:14
  2334.7 91.9 %collective-permute-start.7 = (f32[8,128,16,128]{3,1,2,0:T(8,128)}, f32[8,128,16,128]{3,1,2,0:T(8,128)}, u32[]{:S(2)}, u32[]{:S(2)}) collective-permute-start(f32[8,128,16,128]{3,1,2,0:T(8,128)} %get-tuple-element.115), channel_id=1, source_target_pairs={{0,28},{4,0},{8,4},{12,8},{16,12},{20,16},{24,20},{28,24},{1,29},{... | collective-permute-start | bytes 25165832 | tf_op jit(solution)/shard_map/ppermute | solution.py:14
  2446.6 363.3 %collective-permute-start.8 = (f32[8,128,16,128]{3,1,2,0:T(8,128)}, f32[8,128,16,128]{3,1,2,0:T(8,128)}, u32[]{:S(2)}, u32[]{:S(2)}) collective-permute-start(f32[8,128,16,128]{3,1,2,0:T(8,128)} %get-tuple-element.111), channel_id=1, source_target_pairs={{0,2},{1,3},{2,0},{3,1},{4,6},{5,7},{6,4},{7,5},{8,10},{9,11},{10,... | collective-permute-start | bytes 25165832 | tf_op jit(solution)/shard_map/ppermute | solution.py:14
  2820.0 184.6 %collective-permute-start.9 = (f32[8,128,16,128]{3,1,2,0:T(8,128)}, f32[8,128,16,128]{3,1,2,0:T(8,128)S(1)}, u32[]{:S(2)}, u32[]{:S(2)}) collective-permute-start(f32[8,128,16,128]{3,1,2,0:T(8,128)} %get-tuple-element.109), channel_id=1, source_target_pairs={{0,3},{1,0},{2,1},{3,2},{4,7},{5,4},{6,5},{7,6},{8,11},{9,8},{10,9... | collective-permute-start | bytes 25165832 | tf_op jit(solution)/shard_map/ppermute | solution.py:14
  3023.2 157.3 %all-reduce.22.cloned.1.call-start = ((), (), s32[]{:S(2)}) async-start(), calls=%async_computation.1 | async-start | bytes 2097152 | tf_op jit(solution)/shard_map/psum | solution.py:19
  3124.5 291.5 %all-reduce.20.cloned.1.call-start = ((), (), s32[]{:S(2)}) async-start(), calls=%async_computation | async-start | bytes 8388608 | tf_op jit(solution)/shard_map/psum | solution.py:19
  3335.4 84.3 %copy-start.3 = (f32[1024,512]{1,0:T(8,128)}, f32[1024,512]{1,0:T(8,128)S(1)}, u32[]{:S(2)}) copy-start(f32[1024,512]{1,0:T(8,128)S(1)} %get-tuple-element.221) | copy-start | bytes 6291460
  (16 other events, 39.8 us)
Sparse Core Ops, SparseCore 0:
  19.0 90.7 all-reduce.35
  119.1 55.8 all-reduce.29
  349.0 80.3 all-reduce.27
  1530.8 89.8 all-reduce.33
  1632.2 55.8 all-reduce.25
  1843.3 80.3 all-reduce.23
  3023.3 89.6 all-reduce.31
  3124.6 55.8 all-reduce.21
  3335.6 80.3 all-reduce.19
where the time goes:
time: 3460 us; the launch traced here: 3450 us
  waiting for transfers between devices  2660 us (77%)
  other arithmetic  506 us (15%)
  local copies, waits for them, and re-layouts  129 us (4%)
  matrix products  113 us (3%)
    ppermute x10, waiting for transfers between devices, shifted(): return lax.ppermute(value, axis, pairs)  1990 us
    psum x9, waiting for transfers between devices, spread(): return lax.psum(block, axis)  673 us
    another operation x44, other arithmetic, factor_local(): factor_block = jnp.linalg.cholesky(diagonal)  240 us
    another operation x7, other arithmetic, factor_local(): lax.linalg.triangular_solve(factor_block, jnp.eye(PANEL, dtype=jnp.float3...  121 us
    select_n x10, other arithmetic, relocate(): sending = jnp.where(tile_mask, block_data, 0.0)  105 us
  transfers between devices with their start and end apart: 19, of which 19 were waited for; matrix products, arithmetic and copies ran while one was open for 0% of the time, Pallas kernels for 0%

commit v1 on v0

--- a/solution.py
+++ b/solution.py
@@ -79,22 +79,17 @@
         return front.reshape(tiles_row, tile_size, tiles_col, tile_size)
 
     def factor_local(matrix):
-        first_tile = 0 // tile_size
-        pieces = []
-        for member in range(panel_tiles):
-            global_col = first_tile + member
-            pieces.append(
-                spread(matrix[:, :, global_col // col_count, :], "col", global_col % col_count)
-            )
-        panel_cols = jnp.stack(pieces, axis=2).reshape(tiles_row * tile_size, PANEL)
+        depth = -(-panel_tiles // col_count)
+        gathered = lax.all_gather(matrix[:, :, :depth, :], "col")
+        panel_cols = gathered.transpose(1, 2, 3, 0, 4).reshape(
+            tiles_row * tile_size, depth * col_count * tile_size
+        )[:, :PANEL]
         panel_tiled = panel_cols.reshape(tiles_row, tile_size, PANEL)
-        diagonal_parts = []
-        for member in range(panel_tiles):
-            global_row = first_tile + member
-            diagonal_parts.append(
-                spread(panel_tiled[global_row // row_count], "row", global_row % row_count)
-            )
-        diagonal = jnp.concatenate(diagonal_parts, axis=0)
+        depth = -(-panel_tiles // row_count)
+        gathered = lax.all_gather(panel_tiled[:depth], "row")
+        diagonal = gathered.transpose(1, 0, 2, 3).reshape(
+            depth * row_count * tile_size, PANEL
+        )[:PANEL]
         factor_block = jnp.linalg.cholesky(diagonal)
         inverse = lax.linalg.triangular_solve(
             factor_block, jnp.eye(PANEL, dtype=jnp.float32), left_side=True, lower=True
@@ -124,9 +119,13 @@
         return (lower_panel, schur)
 
     def extend_local(parent, schur, block_map):
-        moved = relocate(schur, block_map, 0, row_count, row_index, shift_rows)
-        moved = relocate(moved, block_map, 2, col_count, col_index, shift_cols)
-        return parent + moved
+        half = tile_size // 2
+        upper, under = schur[:, :half], schur[:, half:]
+        upper = relocate(upper, block_map, 0, row_count, row_index, shift_rows)
+        under = relocate(under, block_map, 2, col_count, col_index, shift_cols)
+        upper = relocate(upper, block_map, 2, col_count, col_index, shift_cols)
+        under = relocate(under, block_map, 0, row_count, row_index, shift_rows)
+        return parent + jnp.concatenate([upper, under], axis=1)
 
     lower_first, schur_first = factor_local(local_form(front_first))
     lower_second, schur_second = factor_local(

time: 3460 us -> 3250 us (0.939)
  waiting for transfers between devices: 2660 us -> 2450 us
    psum x9 -> x3, waiting for transfers between devices: 673 us -> 237 us  [spread(): return lax.psum(block, axis)]
    all_gather x0 -> x6, waiting for transfers between devices: none -> 225 us  [the longest x3 146 us: factor_local(): gathered = lax.all_gather(matrix[:, :, :depth, :], 'col')]
    select_n x10 -> x18, other arithmetic: 105 us -> 126 us  [relocate(): sending = jnp.where(tile_mask, block_data, 0.0)]
    ppermute x10 -> x20, waiting for transfers between devices: 1990 us -> 1990 us  [shifted(): return lax.ppermute(value, axis, pairs)]
  transfers between devices with their start and end apart: 19 -> 29, of which waited for: 19 -> 29; matrix products, arithmetic and copies ran while one was open for 0% -> 0% of each run, Pallas kernels for 0% -> 0%
where the time goes in v1:
time: 3250 us; the launch traced here: 3240 us
  waiting for transfers between devices  2450 us (75%)
  other arithmetic  520 us (16%)
  local copies, waits for them, and re-layouts  122 us (4%)
  matrix products  95.2 us (3%)
    ppermute x20, waiting for transfers between devices, shifted(): return lax.ppermute(value, axis, pairs)  1990 us
    another operation x44, other arithmetic, factor_local(): factor_block = jnp.linalg.cholesky(diagonal)  238 us
    psum x3, waiting for transfers between devices, spread(): return lax.psum(block, axis)  237 us
    all_gather x3, waiting for transfers between devices, factor_local(): gathered = lax.all_gather(matrix[:, :, :depth, :], 'col')  146 us
    select_n x18, other arithmetic, relocate(): sending = jnp.where(tile_mask, block_data, 0.0)  126 us
    another operation x7, other arithmetic, factor_local(): lax.linalg.triangular_solve(factor_block, jnp.eye(PANEL, dtype=jnp.float3...  118 us
    all_gather x3, waiting for transfers between devices, factor_local(): gathered = lax.all_gather(panel_tiled[:depth], 'row')  78.9 us
  transfers between devices with their start and end apart: 29, of which 29 were waited for; matrix products, arithmetic and copies ran while one was open for 0% of the time, Pallas kernels for 0%

profile of v1, /device:TPU:0, one launch (start us, length us, event | category | flops | bytes accessed | tf_op | source)
XLA Modules:
  0.0 3241.5 jit_solution(15788326746258055732)
XLA Ops:
  14.0 48.7 %all-gather.16.cloned.1.call-done = f32[32,128,1,128]{3,1,2,0:T(8,128)} async-done(((f32[8,128,1,128]{3,1,2,0:T(8,128)}), f32[32,128,1,128]{3,1,2,0:T(8,128)}) %all-gather.16.cloned.1.call-update) | async-done | bytes 2097168 | tf_op jit(solution)/shard_map/all_gather | solution.py:83
  250.3 78.7 %all-reduce.12.cloned.1.call-done = (f32[8,1,128,512]{2,0,3,1:T(8,128)}, f32[8,1,128,512]{2,0,3,1:T(8,128)}) async-done(((f32[8,1,128,512]{2,0,3,1:T(8,128)}, f32[8,1,128,512]{2,0,3,1:T(8,128)}), (f32[8,1,128,512]{2,0,3,1:T(8,128)}, f32[8,1,128,512]{2,0,3,1:T(8,128)})) %all-reduce.12.cloned.1.call-update) | async-done | bytes 4194320 | tf_op jit(solution)/shard_map/psum | solution.py:19
  363.5 91.0 %collective-permute-done = f32[8,64,16,128]{3,1,2,0:T(8,128)} collective-permute-done((f32[8,64,16,128]{3,1,2,0:T(8,128)}, f32[8,64,16,128]{3,1,2,0:T(8,128)}, u32[]{:S(2)}, u32[]{:S(2)}) %collective-permute-start) | collective-permute-done | bytes 4194336 | tf_op jit(solution)/shard_map/ppermute | solution.py:14
  465.4 90.0 %collective-permute-done.1 = f32[8,64,16,128]{3,1,2,0:T(8,128)} collective-permute-done((f32[8,64,16,128]{3,1,2,0:T(8,128)}, f32[8,64,16,128]{3,1,2,0:T(8,128)}, u32[]{:S(2)}, u32[]{:S(2)}) %collective-permute-start.1) | collective-permute-done | bytes 4194336 | tf_op jit(solution)/shard_map/ppermute | solution.py:14
  565.1 46.3 %collective-permute-done.2 = f32[8,64,16,128]{3,1,2,0:T(8,128)} collective-permute-done((f32[8,64,16,128]{3,1,2,0:T(8,128)}, f32[8,64,16,128]{3,1,2,0:T(8,128)}, u32[]{:S(2)}, u32[]{:S(2)}) %collective-permute-start.2) | collective-permute-done | bytes 4194336 | tf_op jit(solution)/shard_map/ppermute | solution.py:14
  628.9 270.5 %collective-permute-done.3 = f32[8,64,16,128]{3,1,2,0:T(8,128)} collective-permute-done((f32[8,64,16,128]{3,1,2,0:T(8,128)}, f32[8,64,16,128]{3,1,2,0:T(8,128)}, u32[]{:S(2)}, u32[]{:S(2)}) %collective-permute-start.3) | collective-permute-done | bytes 4194336 | tf_op jit(solution)/shard_map/ppermute | solution.py:14
  899.4 89.9 %collective-permute-done.5 = f32[8,64,16,128]{3,1,2,0:T(8,128)} collective-permute-done((f32[8,64,16,128]{3,1,2,0:T(8,128)}, f32[8,64,16,128]{3,1,2,0:T(8,128)}, u32[]{:S(2)}, u32[]{:S(2)}) %collective-permute-start.5) | collective-permute-done | bytes 4194336 | tf_op jit(solution)/shard_map/ppermute | solution.py:14
  1005.6 91.2 %collective-permute-done.6 = f32[8,64,16,128]{3,1,2,0:T(8,128)} collective-permute-done((f32[8,64,16,128]{3,1,2,0:T(8,128)}, f32[8,64,16,128]{3,1,2,0:T(8,128)}, u32[]{:S(2)}, u32[]{:S(2)}) %collective-permute-start.6) | collective-permute-done | bytes 4194336 | tf_op jit(solution)/shard_map/ppermute | solution.py:14
  1096.8 89.1 %collective-permute-done.4 = f32[8,64,16,128]{3,1,2,0:T(8,128)} collective-permute-done((f32[8,64,16,128]{3,1,2,0:T(8,128)}, f32[8,64,16,128]{3,1,2,0:T(8,128)}, u32[]{:S(2)}, u32[]{:S(2)}) %collective-permute-start.4) | collective-permute-done | bytes 4194336 | tf_op jit(solution)/shard_map/ppermute | solution.py:14
  1194.4 90.8 %collective-permute-done.7 = f32[8,64,16,128]{3,1,2,0:T(8,128)S(1)} collective-permute-done((f32[8,64,16,128]{3,1,2,0:T(8,128)S(1)}, f32[8,64,16,128]{3,1,2,0:T(8,128)S(1)}, u32[]{:S(2)}, u32[]{:S(2)}) %collective-permute-start.7) | collective-permute-done | bytes 4194336 | tf_op jit(solution)/shard_map/ppermute | solution.py:14
  1295.4 88.8 %collective-permute-done.8 = f32[8,64,16,128]{3,1,2,0:T(8,128)S(1)} collective-permute-done((f32[8,64,16,128]{3,1,2,0:T(8,128)}, f32[8,64,16,128]{3,1,2,0:T(8,128)S(1)}, u32[]{:S(2)}, u32[]{:S(2)}) %collective-permute-start.8) | collective-permute-done | bytes 4194336 | tf_op jit(solution)/shard_map/ppermute | solution.py:14
  1451.1 48.9 %all-gather.18.cloned.1.call-done = f32[32,128,1,128]{3,1,2,0:T(8,128)} async-done(((f32[8,128,1,128]{3,1,2,0:T(8,128)}), f32[32,128,1,128]{3,1,2,0:T(8,128)}) %all-gather.18.cloned.1.call-update) | async-done | bytes 2097168 | tf_op jit(solution)/shard_map/all_gather | solution.py:83
  1687.3 79.0 %all-reduce.10.cloned.1.call-done = (f32[8,1,128,512]{2,0,3,1:T(8,128)}, f32[8,1,128,512]{2,0,3,1:T(8,128)}) async-done(((f32[8,1,128,512]{2,0,3,1:T(8,128)}, f32[8,1,128,512]{2,0,3,1:T(8,128)}), (f32[8,1,128,512]{2,0,3,1:T(8,128)}, f32[8,1,128,512]{2,0,3,1:T(8,128)})) %all-reduce.10.cloned.1.call-update) | async-done | bytes 4194320 | tf_op jit(solution)/shard_map/psum | solution.py:19
  1795.5 90.9 %collective-permute-done.10 = f32[8,64,16,128]{3,1,2,0:T(8,128)S(1)} collective-permute-done((f32[8,64,16,128]{3,1,2,0:T(8,128)S(1)}, f32[8,64,16,128]{3,1,2,0:T(8,128)S(1)}, u32[]{:S(2)}, u32[]{:S(2)}) %collective-permute-start.10) | collective-permute-done | bytes 4194336 | tf_op jit(solution)/shard_map/ppermute | solution.py:14
  1891.7 89.8 %collective-permute-done.11 = f32[8,64,16,128]{3,1,2,0:T(8,128)} collective-permute-done((f32[8,64,16,128]{3,1,2,0:T(8,128)S(1)}, f32[8,64,16,128]{3,1,2,0:T(8,128)}, u32[]{:S(2)}, u32[]{:S(2)}) %collective-permute-start.11) | collective-permute-done | bytes 4194336 | tf_op jit(solution)/shard_map/ppermute | solution.py:14
  1989.7 46.3 %collective-permute-done.12 = f32[8,64,16,128]{3,1,2,0:T(8,128)S(1)} collective-permute-done((f32[8,64,16,128]{3,1,2,0:T(8,128)}, f32[8,64,16,128]{3,1,2,0:T(8,128)S(1)}, u32[]{:S(2)}, u32[]{:S(2)}) %collective-permute-start.12) | collective-permute-done | bytes 4194336 | tf_op jit(solution)/shard_map/ppermute | solution.py:14
  2060.3 270.4 %collective-permute-done.13 = f32[8,64,16,128]{3,1,2,0:T(8,128)S(1)} collective-permute-done((f32[8,64,16,128]{3,1,2,0:T(8,128)}, f32[8,64,16,128]{3,1,2,0:T(8,128)S(1)}, u32[]{:S(2)}, u32[]{:S(2)}) %collective-permute-start.13) | collective-permute-done | bytes 4194336 | tf_op jit(solution)/shard_map/ppermute | solution.py:14
  2330.7 89.9 %collective-permute-done.15 = f32[8,64,16,128]{3,1,2,0:T(8,128)S(1)} collective-permute-done((f32[8,64,16,128]{3,1,2,0:T(8,128)}, f32[8,64,16,128]{3,1,2,0:T(8,128)S(1)}, u32[]{:S(2)}, u32[]{:S(2)}) %collective-permute-start.15) | collective-permute-done | bytes 4194336 | tf_op jit(solution)/shard_map/ppermute | solution.py:14
  2435.6 91.2 %collective-permute-done.16 = f32[8,64,16,128]{3,1,2,0:T(8,128)S(1)} collective-permute-done((f32[8,64,16,128]{3,1,2,0:T(8,128)}, f32[8,64,16,128]{3,1,2,0:T(8,128)S(1)}, u32[]{:S(2)}, u32[]{:S(2)}) %collective-permute-start.16) | collective-permute-done | bytes 4194336 | tf_op jit(solution)/shard_map/ppermute | solution.py:14
  2526.8 88.9 %collective-permute-done.14 = f32[8,64,16,128]{3,1,2,0:T(8,128)S(1)} collective-permute-done((f32[8,64,16,128]{3,1,2,0:T(8,128)S(1)}, f32[8,64,16,128]{3,1,2,0:T(8,128)S(1)}, u32[]{:S(2)}, u32[]{:S(2)}) %collective-permute-start.14) | collective-permute-done | bytes 4194336 | tf_op jit(solution)/shard_map/ppermute | solution.py:14
  2625.6 91.0 %collective-permute-done.17 = f32[8,64,16,128]{3,1,2,0:T(8,128)S(1)} collective-permute-done((f32[8,64,16,128]{3,1,2,0:T(8,128)}, f32[8,64,16,128]{3,1,2,0:T(8,128)S(1)}, u32[]{:S(2)}, u32[]{:S(2)}) %collective-permute-start.17) | collective-permute-done | bytes 4194336 | tf_op jit(solution)/shard_map/ppermute | solution.py:14
  2726.7 88.9 %collective-permute-done.18 = f32[8,64,16,128]{3,1,2,0:T(8,128)S(1)} collective-permute-done((f32[8,64,16,128]{3,1,2,0:T(8,128)}, f32[8,64,16,128]{3,1,2,0:T(8,128)S(1)}, u32[]{:S(2)}, u32[]{:S(2)}) %collective-permute-start.18) | collective-permute-done | bytes 4194336 | tf_op jit(solution)/shard_map/ppermute | solution.py:14
  2882.3 48.9 %all-gather.20.cloned.1.call-done = f32[32,128,1,128]{3,1,2,0:T(8,128)} async-done(((f32[8,128,1,128]{3,1,2,0:T(8,128)}), f32[32,128,1,128]{3,1,2,0:T(8,128)}) %all-gather.20.cloned.1.call-update) | async-done | bytes 2097168 | tf_op jit(solution)/shard_map/all_gather | solution.py:83
  3118.4 79.6 %all-reduce.8.cloned.1.call-done = (f32[8,1,128,512]{2,0,3,1:T(8,128)}, f32[8,1,128,512]{2,0,3,1:T(8,128)}) async-done(((f32[8,1,128,512]{2,0,3,1:T(8,128)}, f32[8,1,128,512]{2,0,3,1:T(8,128)}), (f32[8,1,128,512]{2,0,3,1:T(8,128)}, f32[8,1,128,512]{2,0,3,1:T(8,128)})) %all-reduce.8.cloned.1.call-update) | async-done | bytes 4194320 | tf_op jit(solution)/shard_map/psum | solution.py:19
  (312 shorter events, 963.5 us)
Async XLA Ops:
  13.9 78.9 %all-gather.10.cloned.1.call-start = ((), (), s32[]{:S(2)}) async-start(), calls=%async_computation | async-start | bytes 2359296 | tf_op jit(solution)/shard_map/all_gather | solution.py:89
  66.1 262.9 %all-reduce.12.cloned.1.call-start = ((), (), s32[]{:S(2)}) async-start(), calls=%async_computation.8 | async-start | bytes 8388608 | tf_op jit(solution)/shard_map/psum | solution.py:19
  247.6 1252.4 %all-gather.18.cloned.1.call-start = ((), (), s32[]{:S(2)}) async-start(), calls=%async_computation.4 | async-start | bytes 2621440 | tf_op jit(solution)/shard_map/all_gather | solution.py:83
  361.9 92.6 %collective-permute-start = (f32[8,64,16,128]{3,1,2,0:T(8,128)}, f32[8,64,16,128]{3,1,2,0:T(8,128)}, u32[]{:S(2)}, u32[]{:S(2)}) collective-permute-start(f32[8,64,16,128]{3,1,2,0:T(8,128)} %slice_select_fusion.3), channel_id=1, source_target_pairs={{0,16},{4,20},{8,24},{12,28},{16,0},{20,4},{24,8},{28,12},{1,17},{... | collective-permute-start | bytes 12582920 | tf_op jit(solution)/shard_map/ppermute | solution.py:14
  463.6 91.8 %collective-permute-start.1 = (f32[8,64,16,128]{3,1,2,0:T(8,128)}, f32[8,64,16,128]{3,1,2,0:T(8,128)}, u32[]{:S(2)}, u32[]{:S(2)}) collective-permute-start(f32[8,64,16,128]{3,1,2,0:T(8,128)} %get-tuple-element.117), channel_id=1, source_target_pairs={{0,24},{4,28},{8,0},{12,4},{16,8},{20,12},{24,16},{28,20},{1,25},{... | collective-permute-start | bytes 12582920 | tf_op jit(solution)/shard_map/ppermute | solution.py:14
  626.0 273.4 %collective-permute-start.3 = (f32[8,64,16,128]{3,1,2,0:T(8,128)}, f32[8,64,16,128]{3,1,2,0:T(8,128)}, u32[]{:S(2)}, u32[]{:S(2)}) collective-permute-start(f32[8,64,16,128]{3,1,2,0:T(8,128)} %get-tuple-element.111), channel_id=1, source_target_pairs={{0,2},{1,3},{2,0},{3,1},{4,6},{5,7},{6,4},{7,5},{8,10},{9,11},{10,... | collective-permute-start | bytes 12582920 | tf_op jit(solution)/shard_map/ppermute | solution.py:14
  628.4 360.9 %collective-permute-start.5 = (f32[8,64,16,128]{3,1,2,0:T(8,128)}, f32[8,64,16,128]{3,1,2,0:T(8,128)}, u32[]{:S(2)}, u32[]{:S(2)}) collective-permute-start(f32[8,64,16,128]{3,1,2,0:T(8,128)} %get-tuple-element.179), channel_id=1, source_target_pairs={{0,2},{1,3},{2,0},{3,1},{4,6},{5,7},{6,4},{7,5},{8,10},{9,11},{10,... | collective-permute-start | bytes 12582920 | tf_op jit(solution)/shard_map/ppermute | solution.py:14
  1001.3 95.5 %collective-permute-start.6 = (f32[8,64,16,128]{3,1,2,0:T(8,128)}, f32[8,64,16,128]{3,1,2,0:T(8,128)}, u32[]{:S(2)}, u32[]{:S(2)}) collective-permute-start(f32[8,64,16,128]{3,1,2,0:T(8,128)} %get-tuple-element.177), channel_id=1, source_target_pairs={{0,3},{1,0},{2,1},{3,2},{4,7},{5,4},{6,5},{7,6},{8,11},{9,8},{10,9... | collective-permute-start | bytes 12582920 | tf_op jit(solution)/shard_map/ppermute | solution.py:14
  1005.6 180.3 %collective-permute-start.4 = (f32[8,64,16,128]{3,1,2,0:T(8,128)}, f32[8,64,16,128]{3,1,2,0:T(8,128)}, u32[]{:S(2)}, u32[]{:S(2)}) collective-permute-start(f32[8,64,16,128]{3,1,2,0:T(8,128)} %get-tuple-element.109), channel_id=1, source_target_pairs={{0,3},{1,0},{2,1},{3,2},{4,7},{5,4},{6,5},{7,6},{8,11},{9,8},{10,9... | collective-permute-start | bytes 12582920 | tf_op jit(solution)/shard_map/ppermute | solution.py:14
  1193.4 91.8 %collective-permute-start.7 = (f32[8,64,16,128]{3,1,2,0:T(8,128)S(1)}, f32[8,64,16,128]{3,1,2,0:T(8,128)S(1)}, u32[]{:S(2)}, u32[]{:S(2)}) collective-permute-start(f32[8,64,16,128]{3,1,2,0:T(8,128)S(1)} %get-tuple-element.123), channel_id=1, source_target_pairs={{0,16},{4,20},{8,24},{12,28},{16,0},{20,4},{24,8},{28,12},{1,17},{... | collective-permute-start | bytes 12582920 | tf_op jit(solution)/shard_map/ppermute | solution.py:14
  1293.1 91.1 %collective-permute-start.8 = (f32[8,64,16,128]{3,1,2,0:T(8,128)}, f32[8,64,16,128]{3,1,2,0:T(8,128)S(1)}, u32[]{:S(2)}, u32[]{:S(2)}) collective-permute-start(f32[8,64,16,128]{3,1,2,0:T(8,128)} %get-tuple-element.121), channel_id=1, source_target_pairs={{0,24},{4,28},{8,0},{12,4},{16,8},{20,12},{24,16},{28,20},{1,25},{... | collective-permute-start | bytes 12582920 | tf_op jit(solution)/shard_map/ppermute | solution.py:14
  1451.1 79.0 %all-gather.12.cloned.1.call-start = ((), (), s32[]{:S(2)}) async-start(), calls=%async_computation.1 | async-start | bytes 2359296 | tf_op jit(solution)/shard_map/all_gather | solution.py:89
  1503.3 263.0 %all-reduce.10.cloned.1.call-start = ((), (), s32[]{:S(2)}) async-start(), calls=%async_computation.7 | async-start | bytes 8388608 | tf_op jit(solution)/shard_map/psum | solution.py:19
  1685.0 1246.3 %all-gather.20.cloned.1.call-start = ((), (), s32[]{:S(2)}) async-start(), calls=%async_computation.5 | async-start | bytes 2621440 | tf_op jit(solution)/shard_map/all_gather | solution.py:83
  1794.1 92.3 %collective-permute-start.10 = (f32[8,64,16,128]{3,1,2,0:T(8,128)S(1)}, f32[8,64,16,128]{3,1,2,0:T(8,128)S(1)}, u32[]{:S(2)}, u32[]{:S(2)}) collective-permute-start(f32[8,64,16,128]{3,1,2,0:T(8,128)S(1)} %slice_select_fusion.1), channel_id=1, source_target_pairs={{0,16},{4,20},{8,24},{12,28},{16,0},{20,4},{24,8},{28,12},{1,17},{... | collective-permute-start | bytes 12582920 | tf_op jit(solution)/shard_map/ppermute | solution.py:14
  1890.0 91.5 %collective-permute-start.11 = (f32[8,64,16,128]{3,1,2,0:T(8,128)S(1)}, f32[8,64,16,128]{3,1,2,0:T(8,128)}, u32[]{:S(2)}, u32[]{:S(2)}) collective-permute-start(f32[8,64,16,128]{3,1,2,0:T(8,128)S(1)} %get-tuple-element.97), channel_id=1, source_target_pairs={{0,24},{4,28},{8,0},{12,4},{16,8},{20,12},{24,16},{28,20},{1,25},{... | collective-permute-start | bytes 12582920 | tf_op jit(solution)/shard_map/ppermute | solution.py:14
  2057.4 273.3 %collective-permute-start.13 = (f32[8,64,16,128]{3,1,2,0:T(8,128)}, f32[8,64,16,128]{3,1,2,0:T(8,128)S(1)}, u32[]{:S(2)}, u32[]{:S(2)}) collective-permute-start(f32[8,64,16,128]{3,1,2,0:T(8,128)} %get-tuple-element.91), channel_id=1, source_target_pairs={{0,2},{1,3},{2,0},{3,1},{4,6},{5,7},{6,4},{7,5},{8,10},{9,11},{10,... | collective-permute-start | bytes 12582920 | tf_op jit(solution)/shard_map/ppermute | solution.py:14
  2059.8 360.8 %collective-permute-start.15 = (f32[8,64,16,128]{3,1,2,0:T(8,128)}, f32[8,64,16,128]{3,1,2,0:T(8,128)S(1)}, u32[]{:S(2)}, u32[]{:S(2)}) collective-permute-start(f32[8,64,16,128]{3,1,2,0:T(8,128)} %get-tuple-element.175), channel_id=1, source_target_pairs={{0,2},{1,3},{2,0},{3,1},{4,6},{5,7},{6,4},{7,5},{8,10},{9,11},{10,... | collective-permute-start | bytes 12582920 | tf_op jit(solution)/shard_map/ppermute | solution.py:14
  2431.3 95.5 %collective-permute-start.16 = (f32[8,64,16,128]{3,1,2,0:T(8,128)}, f32[8,64,16,128]{3,1,2,0:T(8,128)S(1)}, u32[]{:S(2)}, u32[]{:S(2)}) collective-permute-start(f32[8,64,16,128]{3,1,2,0:T(8,128)} %get-tuple-element.173), channel_id=1, source_target_pairs={{0,3},{1,0},{2,1},{3,2},{4,7},{5,4},{6,5},{7,6},{8,11},{9,8},{10,9... | collective-permute-start | bytes 12582920 | tf_op jit(solution)/shard_map/ppermute | solution.py:14
  2435.5 180.2 %collective-permute-start.14 = (f32[8,64,16,128]{3,1,2,0:T(8,128)S(1)}, f32[8,64,16,128]{3,1,2,0:T(8,128)S(1)}, u32[]{:S(2)}, u32[]{:S(2)}) collective-permute-start(f32[8,64,16,128]{3,1,2,0:T(8,128)S(1)} %get-tuple-element.89), channel_id=1, source_target_pairs={{0,3},{1,0},{2,1},{3,2},{4,7},{5,4},{6,5},{7,6},{8,11},{9,8},{10,9... | collective-permute-start | bytes 12582920 | tf_op jit(solution)/shard_map/ppermute | solution.py:14
  2624.7 92.0 %collective-permute-start.17 = (f32[8,64,16,128]{3,1,2,0:T(8,128)}, f32[8,64,16,128]{3,1,2,0:T(8,128)S(1)}, u32[]{:S(2)}, u32[]{:S(2)}) collective-permute-start(f32[8,64,16,128]{3,1,2,0:T(8,128)} %get-tuple-element.103), channel_id=1, source_target_pairs={{0,16},{4,20},{8,24},{12,28},{16,0},{20,4},{24,8},{28,12},{1,17},{... | collective-permute-start | bytes 12582920 | tf_op jit(solution)/shard_map/ppermute | solution.py:14
  2724.5 91.0 %collective-permute-start.18 = (f32[8,64,16,128]{3,1,2,0:T(8,128)}, f32[8,64,16,128]{3,1,2,0:T(8,128)S(1)}, u32[]{:S(2)}, u32[]{:S(2)}) collective-permute-start(f32[8,64,16,128]{3,1,2,0:T(8,128)} %get-tuple-element.101), channel_id=1, source_target_pairs={{0,24},{4,28},{8,0},{12,4},{16,8},{20,12},{24,16},{28,20},{1,25},{... | collective-permute-start | bytes 12582920 | tf_op jit(solution)/shard_map/ppermute | solution.py:14
  2882.3 79.0 %all-gather.14.cloned.1.call-start = ((), (), s32[]{:S(2)}) async-start(), calls=%async_computation.2 | async-start | bytes 2359296 | tf_op jit(solution)/shard_map/all_gather | solution.py:89
  2934.5 263.4 %all-reduce.8.cloned.1.call-start = ((), (), s32[]{:S(2)}) async-start(), calls=%async_computation.6 | async-start | bytes 8388608 | tf_op jit(solution)/shard_map/psum | solution.py:19
  (28 other events, 410.1 us)
Sparse Core Ops, SparseCore 0:
  14.1 48.6 all-gather.15
  66.2 26.5 all-gather.9
  247.7 81.2 all-reduce.11
  1451.2 48.7 all-gather.17
  1503.4 26.5 all-gather.11
  1685.1 81.1 all-reduce.9
  2882.4 48.7 all-gather.19
  2934.7 26.5 all-gather.13
  3116.7 81.2 all-reduce.7
